TPU v7x, 32 devices: a whole 2x2x4 slice. The times are simulated.
32 devices in a mesh: rep: 4 (over z), tp: 8 (over y, x, core).
Axes of the slice: x: 2, y: 2, z: 4, core: 2. Of those that a mesh axis runs over, the one named last changes fastest.
Arguments:
- hidden: bfloat16 [2048, 4096], P(('rep', 'tp')), may hold values from -6 to 6
- norm_gain: bfloat16 [4096], replicated, may hold values from 0.5 to 1.5
- w_query: bfloat16 [4096, 1024], P(None, 'tp')
- w_key: bfloat16 [4096, 1024], P(None, 'tp'), as said below
- w_value: bfloat16 [4096, 1024], P(None, 'tp'), as said below
- w_output: bfloat16 [4096, 1024], P(None, 'tp'), may hold values from -0.1875 to 0.1875
- kv_pool: bfloat16 [64, 64, 2048], P('rep', None, 'tp'), as said below
- page_table: int32 [32, 2], P('rep'), may hold values from 0 to 15, as said below
- cache_len: int32 [32], P('rep'), may hold values from 1 to 128, as said below
- parents: int32 [32, 64], P('rep'), may hold values from -1 to 62, as said below
- depths: int32 [32, 64], P('rep'), may hold values from 0 to 63, as said below
- accept_node: int32 [32], P('rep'), may hold values from 0 to 63
- migrate_to: int32 [4], replicated, may hold values from 0 to 3, as said below
- leave_slot: int32 [4], replicated, may hold values from 0 to 7
Outputs:
- layer_out: bfloat16 [2048, 4096], P(('rep', 'tp'))
- accepted_kv: bfloat16 [32, 64, 2048], P('rep', None, 'tp')
Inputs may be any that keep to these rules, and one draw needn't show every extreme that they name: `page_table`: each group's rows list each of its 16 pages once. `cache_len`: in each group some slot holds exactly 128 tokens. parents[r, i] < i; node 0 is the root with parent -1. `depths`: the depth of each node in its tree. `migrate_to`: A permutation of the groups that forms one cycle through all of them. `w_key`: the columns of the 4 query heads of one key-value head are equal. `w_value`: the columns of the 4 query heads of one key-value head are equal. `kv_pool`: the 4 heads of one key-value head hold equal keys and values.
All inputs are finite; a program needn't handle non-finite values.
Results may differ from a plain program's by a relative error of at most 0.022.
Values may be sent and summed in bfloat16 or wider, within the bound.
A program may use at most 64 MiB of HBM per device.

v0:
```python
import math

import jax
import jax.numpy as jnp
from jax import lax
from jax.sharding import PartitionSpec as P

eps = 1e-05
rope_base = 1000000.0


def rotate(values_in, positions):
    half = values_in.shape[-1] // 2
    freq = rope_base ** (-(jnp.arange(half, dtype=jnp.float32) * 2.0 / values_in.shape[-1]))
    angle = positions.astype(jnp.float32)[:, None] * freq[None, :]
    cosine = jnp.cos(angle)
    sine = jnp.sin(angle)
    first = values_in[:, :half]
    second = values_in[:, half:]
    return jnp.concatenate(
        [first * cosine - second * sine, second * cosine + first * sine], axis=-1
    )


def ancestors(parents):
    count = parents.shape[-1]
    nodes = jnp.arange(count, dtype=jnp.int32)
    step_up = (parents[..., :, None] == nodes).astype(jnp.float32)
    reach = jnp.eye(count, dtype=jnp.float32) + step_up
    for sweep in range(max(1, (count - 1).bit_length())):
        reach = jnp.minimum(
            jnp.einsum("rij,rjk->rik", reach, reach, precision=lax.Precision.HIGHEST), 1.0
        )
    return reach


def set_terms(query, keys, values, allowed):
    scale = 1.0 / math.sqrt(query.shape[-1])
    scores = jnp.einsum("rqd,rkd->rqk", query, keys, preferred_element_type=jnp.float32) * scale
    scores = jnp.where(allowed, scores, -1e30)
    peak = jnp.max(scores, axis=-1)
    weights = jnp.exp(scores - peak[..., None])
    total = jnp.sum(weights, axis=-1)
    summed = jnp.einsum(
        "rqk,rkd->rqd", weights.astype(jnp.bfloat16), values, preferred_element_type=jnp.float32
    )
    return (peak, total, summed)


def cache_terms(query, cache, lengths):
    head_size = query.shape[-1]
    tokens = jnp.arange(cache.shape[1], dtype=jnp.int32)
    allowed = (tokens[None, :] < lengths[:, None])[:, None, :]
    return set_terms(query, cache[..., :head_size], cache[..., head_size:], allowed)


def local(
    hidden,
    norm_gain,
    w_query,
    w_key,
    w_value,
    w_output,
    kv_pool,
    page_table,
    cache_len,
    parents,
    depths,
    accept_node,
    migrate_to,
    leave_slot,
):
    group_count = lax.axis_size("rep")
    group_index = lax.axis_index("rep")
    residual = hidden.astype(jnp.float32)
    normed = (
        residual
        * lax.rsqrt(jnp.mean(residual * residual, axis=-1, keepdims=True) + eps)
        * norm_gain.astype(jnp.float32)
    ).astype(jnp.bfloat16)
    all_rows = lax.all_gather(normed, "tp", axis=0, tiled=True)
    query = jnp.dot(all_rows, w_query, preferred_element_type=jnp.float32)
    keys_new = jnp.dot(all_rows, w_key, preferred_element_type=jnp.float32)
    values_new = jnp.dot(all_rows, w_value, preferred_element_type=jnp.float32)
    slot_count = cache_len.shape[0]
    draft = parents.shape[1]
    head_size = query.shape[1]
    leaving_slot = leave_slot[group_index]
    source = jnp.sum(
        jnp.arange(group_count, dtype=jnp.int32) * (migrate_to == group_index).astype(jnp.int32)
    )
    moved_lengths = lax.all_gather(cache_len[leaving_slot][None], "rep", axis=0, tiled=True)
    is_arrival = jnp.arange(slot_count, dtype=jnp.int32) == leaving_slot
    new_len = jnp.where(is_arrival, moved_lengths[source], cache_len)
    positions = (new_len[:, None] + depths).reshape(-1)
    q_rot = rotate(query, positions).astype(jnp.bfloat16).reshape(slot_count, draft, head_size)
    k_rot = rotate(keys_new, positions).astype(jnp.bfloat16).reshape(slot_count, draft, head_size)
    v_new = values_new.astype(jnp.bfloat16).reshape(slot_count, draft, head_size)
    own_cache = kv_pool[page_table].reshape(slot_count, -1, 2 * head_size)
    leaving = own_cache[leaving_slot]
    moved = lax.all_gather(leaving[None], "rep", axis=0, tiled=True)
    arrived = moved[source]
    cache = jnp.where(is_arrival[:, None, None], arrived[None], own_cache)
    peak_one, total_one, summed_one = cache_terms(q_rot, cache, new_len)
    ancestry = ancestors(parents)
    peak_two, total_two, summed_two = set_terms(q_rot, k_rot, v_new, ancestry > 0.5)
    peak = jnp.maximum(peak_one, peak_two)
    scale_one = jnp.exp(peak_one - peak)
    scale_two = jnp.exp(peak_two - peak)
    upper = summed_one * scale_one[..., None] + summed_two * scale_two[..., None]
    lower = total_one * scale_one + total_two * scale_two
    attn = (upper / lower[..., None]).astype(jnp.bfloat16).reshape(-1, head_size)
    proj = lax.psum_scatter(
        lax.dot_general(
            attn, w_output, (((1,), (1,)), ((), ())), preferred_element_type=jnp.float32
        ).astype(jnp.bfloat16),
        "tp",
        scatter_dimension=0,
        tiled=True,
    ).astype(jnp.float32)
    layer_out = (residual + proj).astype(jnp.bfloat16)
    on_path = jnp.take_along_axis(ancestry, accept_node[:, None, None], axis=1)[:, 0, :]
    levels = jnp.arange(draft, dtype=jnp.int32)
    select = (
        on_path[:, None, :] * (depths[:, None, :] == levels[None, :, None]).astype(jnp.float32)
    ).astype(jnp.bfloat16)
    kv_rows = jnp.concatenate([k_rot, v_new], axis=-1)
    accepted_kv = jnp.einsum(
        "rji,ric->rjc", select, kv_rows, preferred_element_type=jnp.float32
    ).astype(jnp.bfloat16)
    return (layer_out, accepted_kv)


def solution(mesh):
    in_specs = (
        P(("rep", "tp"), None),
        P(),
        P(None, "tp"),
        P(None, "tp"),
        P(None, "tp"),
        P(None, "tp"),
        P("rep", None, "tp"),
        P("rep", None),
        P("rep"),
        P("rep", None),
        P("rep", None),
        P("rep"),
        P(),
        P(),
    )
    out_specs = (P(("rep", "tp"), None), P("rep", None, "tp"))
    return jax.shard_map(local, mesh=mesh, in_specs=in_specs, out_specs=out_specs, check_vma=False)
```

profile of v0, /device:TPU:0, one launch (start us, length us, event | category | flops | bytes accessed | tf_op | source)
XLA Modules:
  0.0 130.0 jit_solution(7214218450902270450)
XLA Ops:
  7.2 0.0 copy-start
  7.2 0.0 all-gather.2.cloned.1.call-start
  7.2 1.3 %fusion.5 = f32[64]{0:T(128)S(1)} fusion(bf16[64,4096]{1,0:T(8,128)(2,1)} %param.14), kind=kLoop, calls=%fused_computation.23 | loop fusion | flops 786368 | bytes 524544 | tf_op jit(solution)/shard_map/reduce_sum | solution.py:78
  8.6 0.7 convert_element_type.64
  9.3 2.1 %fusion.7 = bf16[64,4096]{1,0:T(8,128)(2,1)} fusion(bf16[64,4096]{1,0:T(8,128)(2,1)} %param.14, f32[4096]{0:T(1024)S(1)} %convert_element_type.64, f32[64]{0:T(128)S(1)} %add_rsqrt_fusion), kind=kLoop, calls=%fused_computation.25 | loop fusion | flops 1048576 | bytes 1065216 | tf_op jit(solution)/shard_map/convert_element_type | solution.py:80
  11.4 0.0 all-gather.2.cloned.1.call-update
  11.4 0.0 reduce-scatter.2.cloned.1.call-start
  11.5 1.2 dynamic_slice.15
  14.0 1.3 dynamic-slice
  15.9 1.4 %dynamic-slice_dynamic-update-slice_fusion = s32[4]{0:T(128)S(1)} fusion(s32[4]{0:T(128)S(1)} %broadcast.103, u32[]{:T(128)} %bitcast.1, s32[8]{0:T(128)} %param.22, s32[]{:T(128)S(6)} %select_n.47), kind=kLoop, calls=%fused_computation.99 | loop fusion | bytes 28
  17.4 9.9 %all-reduce = s32[4]{0:T(128)S(1)} all-reduce(s32[4]{0:T(128)S(1)} %dynamic-slice_dynamic-update-slice_fusion), channel_id=1, replica_groups=mesh['rep'=4,'tp'=8] {'rep'}, use_global_device_ids=true, to_apply=%add | all-reduce | flops 4 | bytes 32
  27.2 1.3 fusion.54
  29.8 0.7 compare_select_fusion
  30.5 0.1 copy.38
  30.6 0.1 reshape.132
  31.3 0.6 dynamic_slice.17
  31.9 1.9 %broadcast_select_fusion.2 = s32[8]{0:T(128)S(1)} fusion(s32[8]{0:T(128)} %param.22, s32[]{:T(128)} %bitcast.2, s32[]{:T(128)} %bitcast), kind=kLoop, calls=%fused_computation.102 | loop fusion | flops 16 | bytes 72 | tf_op jit(solution)/shard_map/jit(_where)/select_n | solution.py:94
  33.8 0.8 add_convert_fusion
  34.5 0.1 convert_element_type.67
  34.6 1.6 %gather_fusion = bf16[16,64,256]{2,1,0:T(8,128)(2,1)S(1)} fusion(bf16[16,64,256]{2,1,0:T(8,128)(2,1)} %param.20, s32[1024]{0:T(1024)S(1)} %pad_clamp_fusion), kind=kCustom, calls=%fused_computation | custom fusion | bytes 1048640 | tf_op jit(solution)/shard_map/gather | solution.py:99
  36.3 13.8 %all_gather.11 = bf16[4,128,256]{2,1,0:T(8,128)(2,1)S(1)} all-gather(bf16[1,128,256]{2,1,0:T(8,128)(2,1)S(1)} %constant_dynamic-slice_fusion), channel_id=1, replica_groups=mesh['rep'=4,'tp'=8] {'rep'}, dimensions={0}, use_global_device_ids=true | all-gather | bytes 327680 | tf_op jit(solution)/shard_map/all_gather | solution.py:101
  50.1 0.7 iota_compare_fusion.5
  50.8 0.1 iota_compare_fusion.4
  50.8 1.3 convolution_minimum_fusion.5
  52.1 0.4 convolution_minimum_fusion.4
  52.5 0.4 convolution_minimum_fusion.3
  52.9 0.4 convolution_minimum_fusion.2
  53.3 0.4 convolution_minimum_fusion.1
  53.7 0.4 fusion.50
  54.1 0.1 and_convert_fusion
  54.2 0.1 broadcast_select_fusion
  54.3 0.0 all-gather.2.cloned.1.call-done
  54.3 0.0 copy-done.3
  54.3 0.0 copy-start.1
  54.4 0.0 copy-start.4
  54.4 3.8 %fusion.65 = f32[512,128]{0,1:T(8,128)S(1)} fusion(bf16[512,4096]{1,0:T(8,128)(2,1)} %all-gather.2.cloned.1.call-done, bf16[4096,128]{1,0:T(8,128)(2,1)S(1)} %copy-done.3), kind=kOutput, calls=%fused_computation.111 | convolution fusion | flops 536870912 | bytes 5505024 | tf_op jit(solution)/shard_map/dot_general | solution.py:83
  58.2 0.0 copy-done.1
  58.2 0.0 copy-done.4
  58.2 1.5 %fusion.64 = f32[512,128]{0,1:T(8,128)S(1)} fusion(bf16[512,4096]{1,0:T(8,128)(2,1)S(1)} %copy-done.1, bf16[4096,128]{1,0:T(8,128)(2,1)S(1)} %copy-done.4), kind=kOutput, calls=%fused_computation.110 | convolution fusion | flops 536870912 | bytes 5505024 | tf_op jit(solution)/shard_map/dot_general | solution.py:82
  59.7 0.6 fusion.35
  60.3 0.1 copy.51
  60.5 0.1 copy.52
  60.6 0.1 copy.50
  60.7 0.1 copy.49
  60.9 0.4 fusion.62
  61.2 0.3 fusion.20
  61.5 0.4 fusion.63
  61.9 0.3 fusion.18
  62.2 0.3 convolution_multiply_fusion.2
  62.5 3.7 %convolution_convert_fusion.2 = bf16[512,128]{1,0:T(8,128)(2,1)S(1)} fusion(bf16[512,4096]{1,0:T(8,128)(2,1)} %all-gather.2.cloned.1.call-done, bf16[4096,128]{1,0:T(8,128)(2,1)} %param.18), kind=kOutput, calls=%fused_computation.22 | convolution fusion | flops 536936448 | bytes 5373952 | tf_op jit(solution)/shard_map/dot_general | solution.py:84
  66.2 0.3 fusion.4
  66.5 0.0 copy-done
  66.5 0.0 copy-start.6
  66.5 0.0 copy-start.5
  66.6 3.2 %convolution_convert_fusion = bf16[512,4096]{1,0:T(8,128)(2,1)} fusion(bf16[512,128]{1,0:T(8,128)(2,1)S(1)} %bitcast.49, bf16[4096,128]{1,0:T(8,128)(2,1)S(1)} %copy-done), kind=kOutput, calls=%fused_computation.2 | convolution fusion | flops 538968064 | bytes 5373952 | tf_op jit(solution)/shard_map/dot_general | solution.py:114
  69.7 0.0 reduce-scatter.2.cloned.1.call-update
  69.8 0.0 copy-done.6
  69.8 0.6 gather_fusion.1
  70.4 0.1 broadcast_select_fusion.1
  70.5 0.0 copy-done.5
  70.5 1.0 convolution_convert_fusion.1
  71.5 49.6 %reduce-scatter.2.cloned.1.call-done = bf16[64,4096]{1,0:T(8,128)(2,1)} async-done(((bf16[512,4096]{1,0:T(8,128)(2,1)}), bf16[64,4096]{1,0:T(8,128)(2,1)}) %reduce-scatter.2.cloned.1.call-update) | async-done | bytes 524304 | tf_op jit(solution)/shard_map/reduce_scatter | solution.py:113
  121.2 0.0 copy-done.2
  121.2 2.0 %fusion.8 = bf16[64,4096]{1,0:T(8,128)(2,1)} fusion(bf16[64,4096]{1,0:T(8,128)(2,1)S(1)} %copy-done.2, bf16[64,4096]{1,0:T(8,128)(2,1)} %reduce-scatter.2.cloned.1.call-done), kind=kLoop, calls=%fused_computation.26 | loop fusion | flops 1048576 | bytes 1572864 | tf_op jit(solution)/shard_map/convert_element_type | solution.py:121
  (15 shorter events, 0.1 us)
Async XLA Ops:
  7.2 59.4 %copy-start = (bf16[4096,128]{1,0:T(8,128)(2,1)S(1)}, bf16[4096,128]{1,0:T(8,128)(2,1)}, u32[]{:S(2)}) copy-start(bf16[4096,128]{1,0:T(8,128)(2,1)} %param.19) | copy-start | bytes 3145732
  7.2 47.1 %all-gather.2.cloned.1.call-start = ((), (), s32[]{:S(2)}) async-start(), calls=%async_computation.1 | async-start | bytes 4718592 | tf_op jit(solution)/shard_map/all_gather | solution.py:81
  9.3 45.1 %copy-start.3 = (bf16[4096,128]{1,0:T(8,128)(2,1)S(1)}, bf16[4096,128]{1,0:T(8,128)(2,1)}, u32[]{:S(2)}) copy-start(bf16[4096,128]{1,0:T(8,128)(2,1)} %param.17) | copy-start | bytes 3145732
  11.4 109.8 %reduce-scatter.2.cloned.1.call-start = ((), (), s32[]{:S(2)}) async-start(), calls=%async_computation.2 | async-start | bytes 4718592 | tf_op jit(solution)/shard_map/reduce_scatter | solution.py:113
  54.3 3.9 %copy-start.1 = (bf16[512,4096]{1,0:T(8,128)(2,1)S(1)}, bf16[512,4096]{1,0:T(8,128)(2,1)}, u32[]{:S(2)}) copy-start(bf16[512,4096]{1,0:T(8,128)(2,1)} %all-gather.2.cloned.1.call-done) | copy-start | bytes 12582916
  54.4 3.9 %copy-start.4 = (bf16[4096,128]{1,0:T(8,128)(2,1)S(1)}, bf16[4096,128]{1,0:T(8,128)(2,1)}, u32[]{:S(2)}) copy-start(bf16[4096,128]{1,0:T(8,128)(2,1)} %param.16) | copy-start | bytes 3145732
  66.5 3.2 %copy-start.6 = (s32[8]{0:T(128)S(1)}, s32[8]{0:T(128)}, u32[]{:S(2)}) copy-start(s32[8]{0:T(128)} %param.25) | copy-start | bytes 100
  66.5 4.0 %copy-start.5 = (s32[8,64]{1,0:T(8,128)S(1)}, s32[8,64]{1,0:T(8,128)}, u32[]{:S(2)}) copy-start(s32[8,64]{1,0:T(8,128)} %param.24) | copy-start | bytes 6148
  69.7 51.4 %copy-start.2 = (bf16[64,4096]{1,0:T(8,128)(2,1)S(1)}, bf16[64,4096]{1,0:T(8,128)(2,1)}, u32[]{:S(2)}) copy-start(bf16[64,4096]{1,0:T(8,128)(2,1)} %param.14) | copy-start | bytes 1572868
Sparse Core Ops, SparseCore 0:
  11.5 39.4 all-gather.1
  69.9 51.2 reduce-scatter.1
where the time goes:
time: 131 us; the launch traced here: 130 us
  waiting for transfers between devices  49.7 us (38%)
  blocking collectives  23.7 us (18%)
  between operations  18.2 us (14%)
  matrix products  17.8 us (14%)
  other arithmetic  12.9 us (10%)
  local copies, waits for them, and re-layouts  7.54 us (6%)
    reduce_scatter x1, waiting for transfers between devices, local(): lax.psum_scatter(lax.dot_general(attn, w_output, (((1,), (1,)), ((), ()))...  49.6 us
    all_gather x1, blocking collectives, local(): moved = lax.all_gather(leaving[None], 'rep', axis=0, tiled=True)  13.8 us
    unnamed x1, blocking collectives  9.89 us
    dot_general x1, matrix products, local(): keys_new = jnp.dot(all_rows, w_key, preferred_element_type=jnp.float32)  3.84 us
    dot_general x1, matrix products, local(): values_new = jnp.dot(all_rows, w_value, preferred_element_type=jnp.float32)  3.73 us
    dot_general x6, matrix products, ancestors(): jnp.einsum('rij,rjk->rik', reach, reach, precision=lax.Precision.HIGHEST)  3.24 us
    dot_general x1, matrix products, local(): lax.dot_general(attn, w_output, (((1,), (1,)), ((), ())), preferred_eleme...  3.19 us
    unnamed x18, local copies, waits for them, and re-layouts  2.73 us
  transfers between devices with their start and end apart: 2, of which 1 were waited for; matrix products, arithmetic and copies ran while one was open for 13% of the time, Pallas kernels for 0%

commit v1 on v0

v1 whole, which is shorter than its diff:
```python
import functools
import math

import jax
import jax.numpy as jnp
from jax import lax
from jax.experimental import pallas as pl
from jax.experimental.pallas import tpu as pltpu
from jax.sharding import PartitionSpec as P

eps = 1e-05
rope_base = 1000000.0
MESH = pl.DeviceIdType.MESH
F32 = jnp.float32
BF16 = jnp.bfloat16


def kernel(
    n,
    reps,
    page_table,
    cache_len,
    accept,
    migrate_to,
    leave_slot,
    hidden,
    gain,
    pool,
    parent_col,
    depth_col,
    depth_row,
    freq,
    w_query,
    w_key,
    w_value,
    w_output,
    out,
    accepted,
    rows,
    w_qkv,
    w_out,
    pages,
    moved_len,
    new_len,
    cos_tab,
    sin_tab,
    anc_tab,
    terms,
    pair_in,
    pair_sum,
    rs_in,
    local_sem,
    ag_send,
    ag_recv,
    fw_send,
    fw_recv,
    ps_send,
    ps_recv,
    rs_send,
    rs_recv,
    mg_send,
    mg_recv,
    ml_send,
    ml_recv,
):
    chips = n // 2
    rows_dev, width = hidden.shape
    head = w_out.shape[1]
    slots = accept.shape[0]
    draft = rows.shape[0] // slots
    pair_rows = 2 * draft
    pairs = slots // 2
    pool_pages = pool.shape[0]
    rep = lax.axis_index("rep")
    me = lax.axis_index("tp")
    core = me % 2
    chip = me // 2
    sibling = chip * 2 + (1 - core)

    def dst_chip(d):
        if chips == 4:
            return ((chip // 2 + d // 2) % 2) * 2 + (chip % 2 + d % 2) % 2
        return (chip + d) % chips

    def src_chip(d):
        if chips == 4:
            return dst_chip(d)
        return (chip + chips - d) % chips

    def block(ref, dev):
        return ref.at[pl.ds(pl.multiple_of(dev * rows_dev, rows_dev), rows_dev), :]

    def remote(src, dst, send, recv, where):
        return pltpu.make_async_remote_copy(
            src_ref=src, dst_ref=dst, send_sem=send, recv_sem=recv,
            device_id=where, device_id_type=MESH,
        )

    loads = [
        pltpu.make_async_copy(w_query, w_qkv.at[:, pl.ds(0, head)], local_sem.at[0]),
        pltpu.make_async_copy(w_key, w_qkv.at[:, pl.ds(head, head)], local_sem.at[1]),
        pltpu.make_async_copy(w_value, w_qkv.at[:, pl.ds(2 * head, head)], local_sem.at[2]),
        pltpu.make_async_copy(w_output, w_out, local_sem.at[3]),
        pltpu.make_async_copy(pool, pages.at[pl.ds(0, pool_pages)], local_sem.at[4]),
    ]
    barrier = pltpu.get_barrier_semaphore()
    pl.semaphore_signal(barrier, inc=1, device_id={"tp": sibling}, device_id_type=MESH)
    for d in range(1, chips):
        pl.semaphore_signal(
            barrier, inc=1, device_id={"tp": dst_chip(d) * 2 + core}, device_id_type=MESH
        )
    for e in range(1, reps):
        pl.semaphore_signal(
            barrier, inc=1, device_id={"rep": (rep + e) % reps}, device_id_type=MESH
        )
    for load in loads:
        load.start()

    own = pl.multiple_of(me * rows_dev, rows_dev)

    @pl.loop(0, rows_dev // 16)
    def _(i):
        x = hidden[pl.ds(pl.multiple_of(i * 16, 16), 16), :].astype(F32)
        mean = jnp.mean(x * x, axis=-1, keepdims=True)
        y = x * lax.rsqrt(mean + eps) * gain[...].astype(F32)
        rows[pl.ds(pl.multiple_of(own + i * 16, 16), 16), :] = y.astype(BF16)

    leaving = leave_slot[rep]
    tail = pool_pages + 2 * rep
    pages[tail] = pool[page_table[leaving, 0]]
    pages[tail + 1] = pool[page_table[leaving, 1]]
    moved_len[rep] = jnp.full(moved_len.shape[1:], cache_len[leaving], jnp.int32)

    pl.semaphore_wait(barrier, 1 + (chips - 1) + (reps - 1))

    gathers = [
        remote(block(rows, me), block(rows, me), ag_send.at[0], ag_recv.at[0], {"tp": sibling})
    ]
    for d in range(1, chips):
        gathers.append(
            remote(
                block(rows, me), block(rows, me), ag_send.at[d], ag_recv.at[d],
                {"tp": dst_chip(d) * 2 + core},
            )
        )
    for d in list(range(1, chips)) + [0]:
        gathers[d].start()
    moves = []
    for e in range(1, reps):
        to = {"rep": (rep + e) % reps}
        moves.append(
            remote(moved_len.at[rep], moved_len.at[rep], ml_send.at[e], ml_recv.at[e], to)
        )
        moves.append(
            remote(
                pages.at[pl.ds(tail, 2)], pages.at[pl.ds(tail, 2)], mg_send.at[e],
                mg_recv.at[e], to,
            )
        )
    for move in moves:
        move.start()

    row_id = lax.broadcasted_iota(jnp.int32, (pair_rows, pair_rows), 0)
    col_id = lax.broadcasted_iota(jnp.int32, (pair_rows, pair_rows), 1)
    reach = []
    for p in range(pairs):
        above = parent_col[p * pair_rows : (p + 1) * pair_rows, :]
        reach.append(((col_id == above) | (col_id == row_id)).astype(F32))
    for sweep in range(max(1, (draft - 1).bit_length())):
        for p in range(pairs):
            low = reach[p].astype(BF16)
            reach[p] = jnp.minimum(jnp.dot(low, low, preferred_element_type=F32), 1.0)
    for p in range(pairs):
        anc_tab[p] = reach[p]

    for move in moves:
        move.wait()
    loads[4].wait()
    source = jnp.int32(0)
    for g in range(reps):
        source = jnp.where(migrate_to[g] == rep, g, source)
    came = moved_len[source][0:1, :]
    half_sign = jnp.where(
        lax.broadcasted_iota(jnp.int32, (1, head), 1) < head // 2, -1.0, 1.0
    ).astype(F32)
    for r in range(slots):
        is_new = (leaving == r).astype(jnp.int32)
        length = came * is_new + cache_len[r] * (1 - is_new)
        new_len[r] = length
        place = (length + depth_col[r * draft : (r + 1) * draft, :]).astype(F32)
        angle = place * freq[...]
        cos_tab[r * draft : (r + 1) * draft, :] = jnp.cos(angle)
        sin_tab[r * draft : (r + 1) * draft, :] = jnp.sin(angle) * half_sign
    for load in loads[:4]:
        load.wait()

    scale = 1.0 / math.sqrt(head)
    token = lax.broadcasted_iota(jnp.int32, (draft, 2 * pages.shape[1]), 1)
    forwards = []

    def arrive(d):
        gathers[d].wait_recv()
        held = block(rows, src_chip(d) * 2 + core)
        forward = remote(held, held, fw_send.at[d], fw_recv.at[d], {"tp": sibling})
        forward.start()
        forwards.append(forward)

    def attend(p):
        first_row = pl.multiple_of(p * pair_rows, pair_rows)
        span = pl.ds(first_row, pair_rows)
        qkv = jnp.dot(rows[span, :], w_qkv[...], preferred_element_type=F32)
        cos = cos_tab[span, :]
        sin = sin_tab[span, :]
        q = qkv[:, :head]
        k = qkv[:, head : 2 * head]
        q = (q * cos + pltpu.roll(q, head // 2, 1) * sin).astype(BF16)
        k = (k * cos + pltpu.roll(k, head // 2, 1) * sin).astype(BF16)
        v = qkv[:, 2 * head :].astype(BF16)
        ancestry = anc_tab[p]
        nt = (((1,), (1,)), ((), ()))
        tree = lax.dot_general(q, k, nt, preferred_element_type=F32) * scale
        tree = jnp.where(ancestry > 0.5, tree, -1e30)
        attn = []
        for part in range(2):
            r = 2 * p + part
            at = slice(part * draft, (part + 1) * draft)
            is_new = (leaving == r).astype(jnp.int32)
            cache = jnp.concatenate(
                [
                    pages[
                        page_table[r, j] * (1 - is_new)
                        + (pool_pages + 2 * source + j) * is_new
                    ]
                    for j in range(2)
                ],
                axis=0,
            )
            cached = lax.dot_general(
                q[at], cache[:, :head], nt, preferred_element_type=F32
            ) * scale
            cached = jnp.where(token < new_len[r], cached, -1e30)
            peak = jnp.maximum(
                jnp.max(cached, axis=-1, keepdims=True),
                jnp.max(tree[at], axis=-1, keepdims=True),
            )
            p_cache = jnp.exp(cached - peak)
            p_tree = jnp.exp(tree[at] - peak)
            total = jnp.sum(p_cache, axis=-1, keepdims=True) + jnp.sum(
                p_tree, axis=-1, keepdims=True
            )
            summed = jnp.dot(
                p_cache.astype(BF16), cache[:, head:], preferred_element_type=F32
            ) + jnp.dot(p_tree.astype(BF16), v, preferred_element_type=F32)
            attn.append((summed / total).astype(BF16))
        attn = jnp.concatenate(attn, axis=0)

        tile = 512

        @pl.loop(0, width // tile)
        def _(i):
            c = pl.ds(pl.multiple_of(i * tile, tile), tile)
            terms[span, c] = lax.dot_general(
                attn, w_out[c, :], nt, preferred_element_type=F32
            ).astype(BF16)

        return (p, k, v, ancestry)

    def accept_path(state):
        p, k, v, ancestry = state
        node = row_id[:, :1]
        chosen = ((node == accept[2 * p]) | (node == accept[2 * p + 1] + draft)).astype(F32)
        on_path = jnp.sum(ancestry * chosen, axis=0, keepdims=True)
        level = depth_row[p] + jnp.where(col_id[:1] < draft, 0, draft)
        select = jnp.where(level == row_id, on_path, 0.0).astype(BF16)
        got_k = jnp.dot(select, k, preferred_element_type=F32).astype(BF16)
        got_v = jnp.dot(select, v, preferred_element_type=F32).astype(BF16)
        for part in range(2):
            at = slice(part * draft, (part + 1) * draft)
            accepted[2 * p + part, :, :head] = got_k[at]
            accepted[2 * p + part, :, head:] = got_v[at]

    swaps = {}

    def swap(d):
        c = src_chip(d)
        swaps[d] = remote(
            block(terms, c * 2 + 1 - core), pair_in.at[c], ps_send.at[d], ps_recv.at[d],
            {"tp": sibling},
        )
        swaps[d].start()

    sends = []

    def pair_and_send(d):
        c = src_chip(d)
        swaps[d].wait_recv()
        base = (c * 2 + core) * rows_dev

        @pl.loop(0, rows_dev // 16)
        def _(i):
            mine = terms[pl.ds(pl.multiple_of(base + i * 16, 16), 16), :].astype(F32)
            at = pl.ds(pl.multiple_of(i * 16, 16), 16)
            pair_sum[c, at, :] = (mine + pair_in[c, at, :].astype(F32)).astype(BF16)

        send = remote(
            pair_sum.at[c], rs_in.at[d], rs_send.at[d], rs_recv.at[d], {"tp": c * 2 + core}
        )
        send.start()
        sends.append(send)

    if chips == pairs:
        gathers[0].wait_recv()
        state = attend(chip)
        swap(0)
        accept_path(state)
        for d in range(1, chips):
            arrive(d)
            forwards[-1].wait_recv()
            state = attend(src_chip(d))
            swap(d)
            accept_path(state)
            pair_and_send(d)
    else:
        gathers[0].wait_recv()
        for d in range(1, chips):
            arrive(d)
        for forward in forwards:
            forward.wait_recv()
        for p in range(pairs):
            accept_path(attend(p))
        for d in range(chips):
            swap(d)
        for d in range(1, chips):
            pair_and_send(d)

    swaps[0].wait_recv()
    for send in sends:
        send.wait_recv()

    @pl.loop(0, rows_dev // 16)
    def _(i):
        at = pl.ds(pl.multiple_of(i * 16, 16), 16)
        total = terms[pl.ds(pl.multiple_of(own + i * 16, 16), 16), :].astype(F32)
        total = total + pair_in[chip, at, :].astype(F32)
        for d in range(1, chips):
            total = total + rs_in[d, at, :].astype(F32)
        out[at, :] = (hidden[at, :].astype(F32) + total).astype(BF16)

    for copy in gathers + forwards + list(swaps.values()) + sends:
        copy.wait_send()


def local(
    n,
    reps,
    hidden,
    norm_gain,
    w_query,
    w_key,
    w_value,
    w_output,
    kv_pool,
    page_table,
    cache_len,
    parents,
    depths,
    accept_node,
    migrate_to,
    leave_slot,
):
    slots, draft = parents.shape
    rows_dev, width = hidden.shape
    head = w_query.shape[1]
    count = slots * draft
    chips = n // 2
    shift = (jnp.arange(slots, dtype=jnp.int32) % 2 * draft)[:, None]
    parent_col = jnp.where(parents >= 0, parents + shift, -1).reshape(count, 1)
    lane = jnp.arange(head, dtype=jnp.int32) % (head // 2)
    freq = (rope_base ** (-(lane.astype(F32) * 2.0 / head)))[None, :]
    smem = pl.BlockSpec(memory_space=pltpu.SMEM)
    vmem = pl.BlockSpec(memory_space=pltpu.VMEM)
    hbm = pl.BlockSpec(memory_space=pl.ANY)
    dma = pltpu.SemaphoreType.DMA
    page = kv_pool.shape[1]
    return pl.pallas_call(
        functools.partial(kernel, n, reps),
        out_shape=(
            jax.ShapeDtypeStruct((rows_dev, width), BF16),
            jax.ShapeDtypeStruct((slots, draft, 2 * head), BF16),
        ),
        in_specs=[smem] * 5 + [vmem] * 7 + [hbm] * 4,
        out_specs=(vmem, vmem),
        scratch_shapes=[
            pltpu.VMEM((count, width), BF16),
            pltpu.VMEM((width, 3 * head), BF16),
            pltpu.VMEM((width, head), BF16),
            pltpu.VMEM((kv_pool.shape[0] + 2 * reps, page, 2 * head), BF16),
            pltpu.VMEM((reps, 8, head), jnp.int32),
            pltpu.VMEM((slots, 1, head), jnp.int32),
            pltpu.VMEM((count, head), F32),
            pltpu.VMEM((count, head), F32),
            pltpu.VMEM((slots // 2, 2 * draft, 2 * draft), F32),
            pltpu.VMEM((count, width), BF16),
            pltpu.VMEM((chips, rows_dev, width), BF16),
            pltpu.VMEM((chips, rows_dev, width), BF16),
            pltpu.VMEM((chips, rows_dev, width), BF16),
            dma((5,)),
        ]
        + [dma((chips,))] * 8
        + [dma((reps,))] * 4,
        compiler_params=pltpu.CompilerParams(
            collective_id=0, has_side_effects=True, vmem_limit_bytes=48 * 1024 * 1024
        ),
    )(
        page_table,
        cache_len,
        accept_node,
        migrate_to,
        leave_slot,
        hidden,
        norm_gain[None, :],
        kv_pool,
        parent_col,
        depths.reshape(count, 1),
        depths.reshape(slots // 2, 1, 2 * draft),
        freq,
        w_query,
        w_key,
        w_value,
        w_output,
    )


def solution(mesh):
    in_specs = (
        P(("rep", "tp"), None),
        P(),
        P(None, "tp"),
        P(None, "tp"),
        P(None, "tp"),
        P(None, "tp"),
        P("rep", None, "tp"),
        P("rep", None),
        P("rep"),
        P("rep", None),
        P("rep", None),
        P("rep"),
        P(),
        P(),
    )
    out_specs = (P(("rep", "tp"), None), P("rep", None, "tp"))
    fn = functools.partial(local, mesh.shape["tp"], mesh.shape["rep"])
    return jax.shard_map(fn, mesh=mesh, in_specs=in_specs, out_specs=out_specs, check_vma=False)
```

time: 131 us -> 68.8 us (0.53)
  Pallas kernels: 0 us -> 57.3 us
  waiting for transfers between devices: 49.7 us -> 0 us
  blocking collectives: 23.7 us -> 0 us
  matrix products: 17.8 us -> 0 us
  between operations: 18.2 us -> 0.76 us
  other arithmetic: 12.9 us -> 0.77 us
  local copies, waits for them, and re-layouts: 7.54 us -> 9.61 us
    pallas_call x0 -> x1, Pallas kernels: none -> 57.3 us  [local(): pl.pallas_call(functools.partial(kernel, n, reps), out_shape=(jax.ShapeDt...]
    reduce_scatter x1 -> x0, waiting for transfers between devices: 49.6 us -> none  [local(): lax.psum_scatter(lax.dot_general(attn, w_output, (((1,), (1,)), ((), ()))...]
    dot_general x15 -> x0, matrix products: 17.8 us -> none  [the longest x1 3.84 us: local(): keys_new = jnp.dot(all_rows, w_key, preferred_element_type=jnp.float32)]
    all_gather x1 -> x0, blocking collectives: 13.8 us -> none  [local(): moved = lax.all_gather(leaving[None], 'rep', axis=0, tiled=True)]
    unnamed x1 -> x0, blocking collectives: 9.89 us -> none
    convert_element_type x5 -> x0, other arithmetic: 5.54 us -> none  [the longest x1 2.11 us: local(): normed = (residual * lax.rsqrt(jnp.mean(residual * residual, axis=-1, kee...]
    unnamed x18 -> x21, local copies, waits for them, and re-layouts: 2.73 us -> 6.99 us
    reduce_sum x4 -> x0, other arithmetic: 3.16 us -> none  [the longest x1 1.32 us: local(): jnp.mean(residual * residual, axis=-1, keepdims=True) + eps]
  transfers between devices with their start and end apart: 2 -> 0, of which waited for: 1 -> 0; matrix products, arithmetic and copies ran while one was open for 13% -> 0% of each run, Pallas kernels for 0% -> 0%
where the time goes in v1:
time: 68.8 us; the launch traced here: 68.4 us
  Pallas kernels  57.3 us (83%)
  local copies, waits for them, and re-layouts  9.61 us (14%)
  other arithmetic  0.77 us (1%)
  between operations  0.76 us (1%)
    pallas_call x1, Pallas kernels, local(): pl.pallas_call(functools.partial(kernel, n, reps), out_shape=(jax.ShapeDt...  57.3 us
    unnamed x21, local copies, waits for them, and re-layouts  6.99 us

profile of v1, /device:TPU:0, one launch (start us, length us, event | category | flops | bytes accessed | tf_op | source)
XLA Modules:
  0.0 68.4 jit_solution(3232816253226672413)
XLA Ops:
  0.6 0.0 copy-start.3
  0.7 0.8 %reshape.59.depth_row = s32[4,1,128]{2,1,0:T(1,128)S(1)} reshape(s32[8,64]{1,0:T(8,128)} %param.24) | data formatting | bytes 4096 | tf_op jit(solution)/shard_map/reshape | solution.py:425
  1.5 0.8 %add_select_fusion = s32[8,64]{1,0:T(8,128)S(1)} fusion(s32[8,64]{1,0:T(8,128)} %param.23, s32[8]{0:T(128)S(1)} %fusion), kind=kLoop, calls=%fused_computation | loop fusion | flops 1536 | bytes 4128 | tf_op jit(solution)/shard_map/jit(_where)/select_n | solution.py:377
  2.2 0.8 %copy.17.page_table = s32[8,2]{1,0:T(8,128)S(1)} copy(s32[8,2]{0,1:T(2,128)} %param.21) | data formatting | bytes 128 | tf_op args[7]
  3.0 0.7 %broadcast_in_dim.9.gain = bf16[1,4096]{1,0:T(2,128)(2,1)S(1)} reshape(bf16[4096]{0:T(1024)(128)(2,1)} %param.15) | data formatting | bytes 16384 | tf_op jit(solution)/shard_map/broadcast_in_dim | solution.py:421
  3.7 0.2 reshape.60.parent_col
  3.9 0.0 copy-start.5
  3.9 0.0 copy-start.6
  3.9 0.0 copy-start.7
  3.9 0.0 copy-start.8
  4.0 0.9 %reshape.61.depth_col = s32[512,1]{1,0:T(8,128)S(1)} reshape(s32[8,64]{1,0:T(8,128)} %param.24) | data formatting | bytes 4096 | tf_op jit(solution)/shard_map/reshape | solution.py:424
  4.9 0.0 copy-done.3
  4.9 0.0 copy-done.5
  4.9 0.0 copy-done.6
  4.9 0.0 copy-done.7
  4.9 0.0 copy-done.8
  4.9 0.0 copy-start
  4.9 1.2 %copy-done = bf16[4096,128]{1,0:T(8,128)(2,1)S(1)} copy-done((bf16[4096,128]{1,0:T(8,128)(2,1)S(1)}, bf16[4096,128]{1,0:T(8,128)(2,1)}, u32[]{:S(2)}) %copy-start) | copy-done | bytes 1048600
  6.1 0.0 copy-start.1
  6.1 1.2 %copy-done.1 = bf16[4096,128]{1,0:T(8,128)(2,1)S(1)} copy-done((bf16[4096,128]{1,0:T(8,128)(2,1)S(1)}, bf16[4096,128]{1,0:T(8,128)(2,1)}, u32[]{:S(2)}) %copy-start.1) | copy-done | bytes 1048600
  7.4 0.0 copy-start.2
  7.4 1.2 %copy-done.2 = bf16[4096,128]{1,0:T(8,128)(2,1)S(1)} copy-done((bf16[4096,128]{1,0:T(8,128)(2,1)S(1)}, bf16[4096,128]{1,0:T(8,128)(2,1)}, u32[]{:S(2)}) %copy-start.2) | copy-done | bytes 1048600
  8.6 0.0 copy-start.4
  8.6 1.0 %copy-done.4 = bf16[16,64,256]{2,1,0:T(8,128)(2,1)S(1)} copy-done((bf16[16,64,256]{2,1,0:T(8,128)(2,1)S(1)}, bf16[16,64,256]{2,1,0:T(8,128)(2,1)}, u32[]{:S(2)}) %copy-start.4) | copy-done | bytes 524312
  9.6 57.3 %shard_map.149 = (bf16[64,4096]{1,0:T(8,128)(2,1)S(1)}, bf16[8,64,256]{2,1,0:T(8,128)(2,1)S(1)}) custom-call(s32[8,2]{1,0:T(8,128)S(1)} %copy.17.page_table, s32[8]{0:T(128)S(1)} %copy-done.5, s32[8]{0:T(128)S(1)} %copy-done.6, s32[4]{0:T(128)S(1)} %copy-done.7, s32[4]{0:T(128)S(1)} %copy-done.8, bf16[64,4096]{1,0:T(8,128)(2,1)S(1)} %copy-done.3, ...), custom_call_target="tpu_custom_call" | custom-call | tf_op jit(solution)/shard_map/pallas_call | solution.py:385
  66.9 0.8 %copy.22 = bf16[64,4096]{1,0:T(8,128)(2,1)} copy(bf16[64,4096]{1,0:T(8,128)(2,1)S(1)} %get-tuple-element.4) | data formatting | bytes 1048576
  67.7 0.7 %copy.23 = bf16[8,64,256]{2,1,0:T(8,128)(2,1)} copy(bf16[8,64,256]{2,1,0:T(8,128)(2,1)S(1)} %get-tuple-element.5) | data formatting | bytes 524288
  (2 shorter events, 0.0 us)
Async XLA Ops:
  0.6 4.2 %copy-start.3 = (bf16[64,4096]{1,0:T(8,128)(2,1)S(1)}, bf16[64,4096]{1,0:T(8,128)(2,1)}, u32[]{:S(2)}) copy-start(bf16[64,4096]{1,0:T(8,128)(2,1)} %hidden.1) | copy-start | bytes 1572868
  3.9 1.0 %copy-start.5 = (s32[8]{0:T(128)S(1)}, s32[8]{0:T(128)}, u32[]{:S(2)}) copy-start(s32[8]{0:T(128)} %cache_len.1) | copy-start | bytes 100
  3.9 1.0 %copy-start.6 = (s32[8]{0:T(128)S(1)}, s32[8]{0:T(128)}, u32[]{:S(2)}) copy-start(s32[8]{0:T(128)} %accept.1) | copy-start | bytes 100
  3.9 1.0 %copy-start.7 = (s32[4]{0:T(128)S(1)}, s32[4]{0:T(128)}, u32[]{:S(2)}) copy-start(s32[4]{0:T(128)} %migrate_to.1) | copy-start | bytes 52
  3.9 1.0 %copy-start.8 = (s32[4]{0:T(128)S(1)}, s32[4]{0:T(128)}, u32[]{:S(2)}) copy-start(s32[4]{0:T(128)} %leave_slot.1) | copy-start | bytes 52
  4.9 1.2 %copy-start = (bf16[4096,128]{1,0:T(8,128)(2,1)S(1)}, bf16[4096,128]{1,0:T(8,128)(2,1)}, u32[]{:S(2)}) copy-start(bf16[4096,128]{1,0:T(8,128)(2,1)} %w_query.1) | copy-start | bytes 3145732
  6.1 1.2 %copy-start.1 = (bf16[4096,128]{1,0:T(8,128)(2,1)S(1)}, bf16[4096,128]{1,0:T(8,128)(2,1)}, u32[]{:S(2)}) copy-start(bf16[4096,128]{1,0:T(8,128)(2,1)} %w_key.1) | copy-start | bytes 3145732
  7.4 1.2 %copy-start.2 = (bf16[4096,128]{1,0:T(8,128)(2,1)S(1)}, bf16[4096,128]{1,0:T(8,128)(2,1)}, u32[]{:S(2)}) copy-start(bf16[4096,128]{1,0:T(8,128)(2,1)} %w_value.1) | copy-start | bytes 3145732
  8.6 1.0 %copy-start.4 = (bf16[16,64,256]{2,1,0:T(8,128)(2,1)S(1)}, bf16[16,64,256]{2,1,0:T(8,128)(2,1)}, u32[]{:S(2)}) copy-start(bf16[16,64,256]{2,1,0:T(8,128)(2,1)} %pool.1) | copy-start | bytes 1572868

commit v2 on v1

--- a/solution.py
+++ b/solution.py
@@ -18,18 +18,17 @@
 def kernel(
     n,
     reps,
-    page_table,
-    cache_len,
-    accept,
-    migrate_to,
-    leave_slot,
     hidden,
     gain,
     pool,
-    parent_col,
-    depth_col,
-    depth_row,
+    parents,
+    depths,
     freq,
+    page_table_in,
+    cache_len_in,
+    accept_in,
+    migrate_to_in,
+    leave_slot_in,
     w_query,
     w_key,
     w_value,
@@ -45,6 +44,12 @@
     cos_tab,
     sin_tab,
     anc_tab,
+    page_table,
+    cache_len,
+    accept,
+    migrate_to,
+    leave_slot,
+    depth_row,
     terms,
     pair_in,
     pair_sum,
@@ -66,7 +71,7 @@
     chips = n // 2
     rows_dev, width = hidden.shape
     head = w_out.shape[1]
-    slots = accept.shape[0]
+    slots = parents.shape[0]
     draft = rows.shape[0] // slots
     pair_rows = 2 * draft
     pairs = slots // 2
@@ -76,6 +81,9 @@
     core = me % 2
     chip = me // 2
     sibling = chip * 2 + (1 - core)
+    grid4 = chips == 4 and slots == 2 * chips
+    first = 1 + core
+    second = 2 - core
 
     def dst_chip(d):
         if chips == 4:
@@ -103,6 +111,13 @@
         pltpu.make_async_copy(w_output, w_out, local_sem.at[3]),
         pltpu.make_async_copy(pool, pages.at[pl.ds(0, pool_pages)], local_sem.at[4]),
     ]
+    small = [
+        pltpu.make_async_copy(page_table_in, page_table, local_sem.at[5]),
+        pltpu.make_async_copy(cache_len_in, cache_len, local_sem.at[6]),
+        pltpu.make_async_copy(accept_in, accept, local_sem.at[7]),
+        pltpu.make_async_copy(migrate_to_in, migrate_to, local_sem.at[8]),
+        pltpu.make_async_copy(leave_slot_in, leave_slot, local_sem.at[9]),
+    ]
     barrier = pltpu.get_barrier_semaphore()
     pl.semaphore_signal(barrier, inc=1, device_id={"tp": sibling}, device_id_type=MESH)
     for d in range(1, chips):
@@ -113,7 +128,7 @@
         pl.semaphore_signal(
             barrier, inc=1, device_id={"rep": (rep + e) % reps}, device_id_type=MESH
         )
-    for load in loads:
+    for load in small + loads:
         load.start()
 
     own = pl.multiple_of(me * rows_dev, rows_dev)
@@ -125,6 +140,8 @@
         y = x * lax.rsqrt(mean + eps) * gain[...].astype(F32)
         rows[pl.ds(pl.multiple_of(own + i * 16, 16), 16), :] = y.astype(BF16)
 
+    for load in small:
+        load.wait()
     leaving = leave_slot[rep]
     tail = pool_pages + 2 * rep
     pages[tail] = pool[page_table[leaving, 0]]
@@ -136,14 +153,15 @@
     gathers = [
         remote(block(rows, me), block(rows, me), ag_send.at[0], ag_recv.at[0], {"tp": sibling})
     ]
-    for d in range(1, chips):
+    for d in range(1, 3 if grid4 else chips):
+        way = (first if d == 1 else second) if grid4 else d
         gathers.append(
             remote(
                 block(rows, me), block(rows, me), ag_send.at[d], ag_recv.at[d],
-                {"tp": dst_chip(d) * 2 + core},
-            )
-        )
-    for d in list(range(1, chips)) + [0]:
+                {"tp": dst_chip(way) * 2 + core},
+            )
+        )
+    for d in [1, 0] if grid4 else list(range(1, chips)) + [0]:
         gathers[d].start()
     moves = []
     for e in range(1, reps):
@@ -163,15 +181,28 @@
     row_id = lax.broadcasted_iota(jnp.int32, (pair_rows, pair_rows), 0)
     col_id = lax.broadcasted_iota(jnp.int32, (pair_rows, pair_rows), 1)
     reach = []
+    place_col = []
     for p in range(pairs):
-        above = parent_col[p * pair_rows : (p + 1) * pair_rows, :]
-        reach.append(((col_id == above) | (col_id == row_id)).astype(F32))
+        above = parents[2 * p + 1 : 2 * p + 2, :]
+        above = jnp.concatenate(
+            [parents[2 * p : 2 * p + 1, :], jnp.where(above >= 0, above + draft, above)], axis=1
+        )
+        reach.append(((row_id == above) | (col_id == row_id)).astype(F32))
+        level = jnp.concatenate(
+            [depths[2 * p : 2 * p + 1, :], depths[2 * p + 1 : 2 * p + 2, :]], axis=1
+        )
+        depth_row[p] = level
+        place_col.append(
+            jnp.sum(
+                jnp.where(row_id == col_id, level.astype(F32), 0.0), axis=1, keepdims=True
+            )
+        )
     for sweep in range(max(1, (draft - 1).bit_length())):
         for p in range(pairs):
             low = reach[p].astype(BF16)
             reach[p] = jnp.minimum(jnp.dot(low, low, preferred_element_type=F32), 1.0)
     for p in range(pairs):
-        anc_tab[p] = reach[p]
+        anc_tab[p] = reach[p].T
 
     for move in moves:
         move.wait()
@@ -187,10 +218,24 @@
         is_new = (leaving == r).astype(jnp.int32)
         length = came * is_new + cache_len[r] * (1 - is_new)
         new_len[r] = length
-        place = (length + depth_col[r * draft : (r + 1) * draft, :]).astype(F32)
+        at = slice(r % 2 * draft, (r % 2 + 1) * draft)
+        place = length.astype(F32) + place_col[r // 2][at]
         angle = place * freq[...]
         cos_tab[r * draft : (r + 1) * draft, :] = jnp.cos(angle)
         sin_tab[r * draft : (r + 1) * draft, :] = jnp.sin(angle) * half_sign
+    hops = []
+    if grid4:
+        gathers[1].wait_send()
+        gathers[2].start()
+        gathers[1].wait_recv()
+        held = block(rows, dst_chip(first) * 2 + core)
+        hops.append(
+            remote(
+                held, held, ag_send.at[3], ag_recv.at[3],
+                {"tp": dst_chip(second) * 2 + core},
+            )
+        )
+        hops[0].start()
     for load in loads[:4]:
         load.wait()
 
@@ -199,8 +244,14 @@
     forwards = []
 
     def arrive(d):
-        gathers[d].wait_recv()
-        held = block(rows, src_chip(d) * 2 + core)
+        if not grid4:
+            gathers[d].wait_recv()
+        elif d == 2:
+            gathers[2].wait_recv()
+        elif d == 3:
+            hops[0].wait_recv()
+        way = {1: first, 2: second, 3: 3}[d] if grid4 else d
+        held = block(rows, src_chip(way) * 2 + core)
         forward = remote(held, held, fw_send.at[d], fw_recv.at[d], {"tp": sibling})
         forward.start()
         forwards.append(forward)
@@ -308,18 +359,65 @@
         send.start()
         sends.append(send)
 
-    if chips == pairs:
+    half = rows_dev // 2
+
+    def add_up(c, start, count, relay):
+        base = (c * 2 + core) * rows_dev
+
+        @pl.loop(0, count // 16)
+        def _(i):
+            total = terms[
+                pl.ds(pl.multiple_of(base + start + i * 16, 16), 16), :
+            ].astype(F32)
+            at = pl.ds(pl.multiple_of(start + i * 16, 16), 16)
+            total = total + pair_in[c, at, :].astype(F32)
+            if relay:
+                total = total + rs_in[3, at, :].astype(F32)
+            pair_sum[c, at, :] = total.astype(BF16)
+
+    def post(c, slot, start, count, sem, way):
+        at = pl.ds(start, count)
+        sends.append(
+            remote(
+                pair_sum.at[c, at, :], rs_in.at[slot, at, :], rs_send.at[sem],
+                rs_recv.at[sem], {"tp": dst_chip(way) * 2 + core},
+            )
+        )
+        sends[-1].start()
+
+    if grid4:
+        near, far, across = dst_chip(first), dst_chip(second), dst_chip(3)
+        arrive(1)
         gathers[0].wait_recv()
         state = attend(chip)
         swap(0)
         accept_path(state)
-        for d in range(1, chips):
-            arrive(d)
-            forwards[-1].wait_recv()
+        arrive(2)
+        for forward in forwards:
+            forward.wait_recv()
+        for d in (1, 2):
             state = attend(src_chip(d))
             swap(d)
             accept_path(state)
-            pair_and_send(d)
+        arrive(3)
+        for d in (1, 2):
+            swaps[d].wait_recv()
+        add_up(near, 0, rows_dev, False)
+        post(near, 1, 0, rows_dev, 1, first)
+        forwards[2].wait_recv()
+        state = attend(across)
+        swap(3)
+        swaps[3].wait_recv()
+        for part in range(2):
+            add_up(across, part * half, half, False)
+            post(across, 3, part * half, half, 3 + part, first)
+        relays = sends[1:3]
+        accept_path(state)
+        for part in range(2):
+            relays[part].wait_recv()
+            add_up(far, part * half, half, True)
+            post(far, 2, part * half, half, (2, 5)[part], second)
+        last = [sends[0], sends[3], sends[4]]
     else:
         gathers[0].wait_recv()
         for d in range(1, chips):
@@ -332,9 +430,10 @@
             swap(d)
         for d in range(1, chips):
             pair_and_send(d)
+        last = sends
 
     swaps[0].wait_recv()
-    for send in sends:
+    for send in last:
         send.wait_recv()
 
     @pl.loop(0, rows_dev // 16)
@@ -342,11 +441,12 @@
         at = pl.ds(pl.multiple_of(i * 16, 16), 16)
         total = terms[pl.ds(pl.multiple_of(own + i * 16, 16), 16), :].astype(F32)
         total = total + pair_in[chip, at, :].astype(F32)
-        for d in range(1, chips):
+        for d in range(1, 3 if grid4 else chips):
             total = total + rs_in[d, at, :].astype(F32)
         out[at, :] = (hidden[at, :].astype(F32) + total).astype(BF16)
 
-    for copy in gathers + forwards + list(swaps.values()) + sends:
+    done = gathers[1] if grid4 else None
+    for copy in [g for g in gathers if g is not done] + hops + forwards + list(swaps.values()) + sends:
         copy.wait_send()
 
 
@@ -373,11 +473,8 @@
     head = w_query.shape[1]
     count = slots * draft
     chips = n // 2
-    shift = (jnp.arange(slots, dtype=jnp.int32) % 2 * draft)[:, None]
-    parent_col = jnp.where(parents >= 0, parents + shift, -1).reshape(count, 1)
     lane = jnp.arange(head, dtype=jnp.int32) % (head // 2)
     freq = (rope_base ** (-(lane.astype(F32) * 2.0 / head)))[None, :]
-    smem = pl.BlockSpec(memory_space=pltpu.SMEM)
     vmem = pl.BlockSpec(memory_space=pltpu.VMEM)
     hbm = pl.BlockSpec(memory_space=pl.ANY)
     dma = pltpu.SemaphoreType.DMA
@@ -388,7 +485,7 @@
             jax.ShapeDtypeStruct((rows_dev, width), BF16),
             jax.ShapeDtypeStruct((slots, draft, 2 * head), BF16),
         ),
-        in_specs=[smem] * 5 + [vmem] * 7 + [hbm] * 4,
+        in_specs=[vmem] * 6 + [hbm] * 9,
         out_specs=(vmem, vmem),
         scratch_shapes=[
             pltpu.VMEM((count, width), BF16),
@@ -400,30 +497,36 @@
             pltpu.VMEM((count, head), F32),
             pltpu.VMEM((count, head), F32),
             pltpu.VMEM((slots // 2, 2 * draft, 2 * draft), F32),
+            pltpu.SMEM(page_table.shape, jnp.int32),
+            pltpu.SMEM(cache_len.shape, jnp.int32),
+            pltpu.SMEM(accept_node.shape, jnp.int32),
+            pltpu.SMEM(migrate_to.shape, jnp.int32),
+            pltpu.SMEM(leave_slot.shape, jnp.int32),
+            pltpu.VMEM((slots // 2, 1, 2 * draft), jnp.int32),
             pltpu.VMEM((count, width), BF16),
             pltpu.VMEM((chips, rows_dev, width), BF16),
             pltpu.VMEM((chips, rows_dev, width), BF16),
             pltpu.VMEM((chips, rows_dev, width), BF16),
-            dma((5,)),
+            dma((10,)),
         ]
-        + [dma((chips,))] * 8
+        + [dma((chips,))] * 6
+        + [dma((chips + 2,))] * 2
         + [dma((reps,))] * 4,
         compiler_params=pltpu.CompilerParams(
             collective_id=0, has_side_effects=True, vmem_limit_bytes=48 * 1024 * 1024
         ),
     )(
+        hidden,
+        norm_gain[None, :],
+        kv_pool,
+        parents,
+        depths,
+        freq,
         page_table,
         cache_len,
         accept_node,
         migrate_to,
         leave_slot,
-        hidden,
-        norm_gain[None, :],
-        kv_pool,
-        parent_col,
-        depths.reshape(count, 1),
-        depths.reshape(slots // 2, 1, 2 * draft),
-        freq,
         w_query,
         w_key,
         w_value,

time: 68.8 us -> 62.4 us (0.907)
  Pallas kernels: 57.3 us -> 51.2 us
  other arithmetic: 0.77 us -> 0.01 us
    pallas_call x1, Pallas kernels: 57.3 us -> 51.2 us  [local(): pl.pallas_call(functools.partial(kernel, n, reps), out_shape=(jax.ShapeDt...]
    unnamed x21 -> x29, local copies, waits for them, and re-layouts: 6.99 us -> 9.24 us
    reshape x3 -> x0, local copies, waits for them, and re-layouts: 1.91 us -> none  [the longest x1 0.9 us: local(): depths.reshape(count, 1)]
    select_n x1 -> x0, other arithmetic: 0.76 us -> none  [local(): parent_col = jnp.where(parents >= 0, parents + shift, -1).reshape(count, 1)]
where the time goes in v2:
time: 62.4 us; the launch traced here: 61.9 us
  Pallas kernels  51.2 us (82%)
  local copies, waits for them, and re-layouts  10 us (16%)
  between operations  0.73 us (1%)
    pallas_call x1, Pallas kernels, local(): pl.pallas_call(functools.partial(kernel, n, reps), out_shape=(jax.ShapeDt...  51.2 us
    unnamed x29, local copies, waits for them, and re-layouts  9.24 us

profile of v2, /device:TPU:0, one launch (start us, length us, event | category | flops | bytes accessed | tf_op | source)
XLA Modules:
  0.0 61.9 jit_solution(6087355786044261120)
XLA Ops:
  0.6 0.0 copy-start.12
  0.7 0.7 %copy-done.12 = s32[8,2]{0,1:T(2,128)S(1)} copy-done((s32[8,2]{0,1:T(2,128)S(1)}, s32[8,2]{0,1:T(2,128)}, u32[]{:S(2)}) %copy-start.12) | copy-done | bytes 88
  1.3 0.1 copy.16.page_table_in
  1.4 0.0 copy-start.6
  1.4 0.0 copy-start.7
  1.4 0.0 copy-start.8
  1.4 0.0 copy-start.9
  1.4 0.0 copy-start.10
  1.4 0.0 copy-start.11
  1.4 0.8 %broadcast_in_dim.4.gain = bf16[1,4096]{1,0:T(2,128)(2,1)S(1)} reshape(bf16[4096]{0:T(1024)(128)(2,1)} %param.15) | data formatting | bytes 16384 | tf_op jit(solution)/shard_map/broadcast_in_dim | solution.py:520
  2.2 0.0 copy-done.6
  2.2 0.0 copy-done.7
  2.2 0.0 copy-done.8
  2.2 0.0 copy-done.9
  2.2 0.0 copy-done.10
  2.2 0.0 copy-done.11
  2.3 0.0 copy-start
  2.3 1.2 %copy-done = bf16[4096,128]{1,0:T(8,128)(2,1)S(1)} copy-done((bf16[4096,128]{1,0:T(8,128)(2,1)S(1)}, bf16[4096,128]{1,0:T(8,128)(2,1)}, u32[]{:S(2)}) %copy-start) | copy-done | bytes 1048600
  3.5 0.0 copy-start.1
  3.5 1.2 %copy-done.1 = bf16[4096,128]{1,0:T(8,128)(2,1)S(1)} copy-done((bf16[4096,128]{1,0:T(8,128)(2,1)S(1)}, bf16[4096,128]{1,0:T(8,128)(2,1)}, u32[]{:S(2)}) %copy-start.1) | copy-done | bytes 1048600
  4.7 0.0 copy-start.2
  4.7 1.2 %copy-done.2 = bf16[4096,128]{1,0:T(8,128)(2,1)S(1)} copy-done((bf16[4096,128]{1,0:T(8,128)(2,1)S(1)}, bf16[4096,128]{1,0:T(8,128)(2,1)}, u32[]{:S(2)}) %copy-start.2) | copy-done | bytes 1048600
  5.9 0.0 copy-start.3
  5.9 1.2 %copy-done.3 = bf16[4096,128]{1,0:T(8,128)(2,1)S(1)} copy-done((bf16[4096,128]{1,0:T(8,128)(2,1)S(1)}, bf16[4096,128]{1,0:T(8,128)(2,1)}, u32[]{:S(2)}) %copy-start.3) | copy-done | bytes 1048600
  7.2 0.0 copy-start.4
  7.2 1.0 %copy-done.4 = bf16[64,4096]{1,0:T(8,128)(2,1)S(1)} copy-done((bf16[64,4096]{1,0:T(8,128)(2,1)S(1)}, bf16[64,4096]{1,0:T(8,128)(2,1)}, u32[]{:S(2)}) %copy-start.4) | copy-done | bytes 524312
  8.2 0.0 copy-start.5
  8.2 1.0 %copy-done.5 = bf16[16,64,256]{2,1,0:T(8,128)(2,1)S(1)} copy-done((bf16[16,64,256]{2,1,0:T(8,128)(2,1)S(1)}, bf16[16,64,256]{2,1,0:T(8,128)(2,1)}, u32[]{:S(2)}) %copy-start.5) | copy-done | bytes 524312
  9.2 51.2 %shard_map.149 = (bf16[64,4096]{1,0:T(8,128)(2,1)S(1)}, bf16[8,64,256]{2,1,0:T(8,128)(2,1)S(1)}) custom-call(bf16[64,4096]{1,0:T(8,128)(2,1)S(1)} %copy-done.4, bf16[1,4096]{1,0:T(2,128)(2,1)S(1)} %broadcast_in_dim.4.gain, bf16[16,64,256]{2,1,0:T(8,128)(2,1)S(1)} %copy-done.5, s32[8,64]{1,0:T(8,128)S(1)} %copy-done.6, s32[8,64]{1,0:T(8,128)S(1)} %copy-done.7, ...), custom_call_target="tpu_custom_call" | custom-call | tf_op jit(solution)/shard_map/pallas_call | solution.py:482
  60.4 0.8 %copy.19 = bf16[64,4096]{1,0:T(8,128)(2,1)} copy(bf16[64,4096]{1,0:T(8,128)(2,1)S(1)} %get-tuple-element.4) | data formatting | bytes 1048576
  61.2 0.7 %copy.20 = bf16[8,64,256]{2,1,0:T(8,128)(2,1)} copy(bf16[8,64,256]{2,1,0:T(8,128)(2,1)S(1)} %get-tuple-element.5) | data formatting | bytes 524288
  (1 shorter events, 0.0 us)
Async XLA Ops:
  0.6 0.7 %copy-start.12 = (s32[8,2]{0,1:T(2,128)S(1)}, s32[8,2]{0,1:T(2,128)}, u32[]{:S(2)}) copy-start(s32[8,2]{0,1:T(2,128)} %param.21) | copy-start | bytes 196
  1.4 0.8 %copy-start.6 = (s32[8,64]{1,0:T(8,128)S(1)}, s32[8,64]{1,0:T(8,128)}, u32[]{:S(2)}) copy-start(s32[8,64]{1,0:T(8,128)} %parents.1) | copy-start | bytes 6148
  1.4 0.8 %copy-start.7 = (s32[8,64]{1,0:T(8,128)S(1)}, s32[8,64]{1,0:T(8,128)}, u32[]{:S(2)}) copy-start(s32[8,64]{1,0:T(8,128)} %depths.1) | copy-start | bytes 6148
  1.4 0.8 %copy-start.8 = (s32[8]{0:T(128)S(1)}, s32[8]{0:T(128)}, u32[]{:S(2)}) copy-start(s32[8]{0:T(128)} %cache_len_in.1) | copy-start | bytes 100
  1.4 0.8 %copy-start.9 = (s32[8]{0:T(128)S(1)}, s32[8]{0:T(128)}, u32[]{:S(2)}) copy-start(s32[8]{0:T(128)} %accept_in.1) | copy-start | bytes 100
  1.4 0.8 %copy-start.10 = (s32[4]{0:T(128)S(1)}, s32[4]{0:T(128)}, u32[]{:S(2)}) copy-start(s32[4]{0:T(128)} %migrate_to_in.1) | copy-start | bytes 52
  1.4 0.8 %copy-start.11 = (s32[4]{0:T(128)S(1)}, s32[4]{0:T(128)}, u32[]{:S(2)}) copy-start(s32[4]{0:T(128)} %leave_slot_in.1) | copy-start | bytes 52
  2.3 1.2 %copy-start = (bf16[4096,128]{1,0:T(8,128)(2,1)S(1)}, bf16[4096,128]{1,0:T(8,128)(2,1)}, u32[]{:S(2)}) copy-start(bf16[4096,128]{1,0:T(8,128)(2,1)} %w_query.1) | copy-start | bytes 3145732
  3.5 1.2 %copy-start.1 = (bf16[4096,128]{1,0:T(8,128)(2,1)S(1)}, bf16[4096,128]{1,0:T(8,128)(2,1)}, u32[]{:S(2)}) copy-start(bf16[4096,128]{1,0:T(8,128)(2,1)} %w_key.1) | copy-start | bytes 3145732
  4.7 1.2 %copy-start.2 = (bf16[4096,128]{1,0:T(8,128)(2,1)S(1)}, bf16[4096,128]{1,0:T(8,128)(2,1)}, u32[]{:S(2)}) copy-start(bf16[4096,128]{1,0:T(8,128)(2,1)} %w_value.1) | copy-start | bytes 3145732
  5.9 1.2 %copy-start.3 = (bf16[4096,128]{1,0:T(8,128)(2,1)S(1)}, bf16[4096,128]{1,0:T(8,128)(2,1)}, u32[]{:S(2)}) copy-start(bf16[4096,128]{1,0:T(8,128)(2,1)} %w_output.1) | copy-start | bytes 3145732
  7.2 1.0 %copy-start.4 = (bf16[64,4096]{1,0:T(8,128)(2,1)S(1)}, bf16[64,4096]{1,0:T(8,128)(2,1)}, u32[]{:S(2)}) copy-start(bf16[64,4096]{1,0:T(8,128)(2,1)} %hidden.1) | copy-start | bytes 1572868
  8.2 1.0 %copy-start.5 = (bf16[16,64,256]{2,1,0:T(8,128)(2,1)S(1)}, bf16[16,64,256]{2,1,0:T(8,128)(2,1)}, u32[]{:S(2)}) copy-start(bf16[16,64,256]{2,1,0:T(8,128)(2,1)} %pool.1) | copy-start | bytes 1572868

commit v3 on v2

--- a/solution.py
+++ b/solution.py
@@ -18,12 +18,12 @@
 def kernel(
     n,
     reps,
-    hidden,
     gain,
-    pool,
     parents,
     depths,
     freq,
+    hidden_in,
+    pool_in,
     page_table_in,
     cache_len_in,
     accept_in,
@@ -50,6 +50,9 @@
     migrate_to,
     leave_slot,
     depth_row,
+    hidden,
+    pool,
+    w_out_t,
     terms,
     pair_in,
     pair_sum,
@@ -109,9 +112,10 @@
         pltpu.make_async_copy(w_key, w_qkv.at[:, pl.ds(head, head)], local_sem.at[1]),
         pltpu.make_async_copy(w_value, w_qkv.at[:, pl.ds(2 * head, head)], local_sem.at[2]),
         pltpu.make_async_copy(w_output, w_out, local_sem.at[3]),
-        pltpu.make_async_copy(pool, pages.at[pl.ds(0, pool_pages)], local_sem.at[4]),
+        pltpu.make_async_copy(pool_in, pages.at[pl.ds(0, pool_pages)], local_sem.at[4]),
     ]
     small = [
+        pltpu.make_async_copy(pool_in, pool, local_sem.at[10]),
         pltpu.make_async_copy(page_table_in, page_table, local_sem.at[5]),
         pltpu.make_async_copy(cache_len_in, cache_len, local_sem.at[6]),
         pltpu.make_async_copy(accept_in, accept, local_sem.at[7]),
@@ -128,8 +132,10 @@
         pl.semaphore_signal(
             barrier, inc=1, device_id={"rep": (rep + e) % reps}, device_id_type=MESH
         )
-    for load in small + loads:
+    load_hidden = pltpu.make_async_copy(hidden_in, hidden, local_sem.at[11])
+    for load in [load_hidden] + small + loads:
         load.start()
+    load_hidden.wait()
 
     own = pl.multiple_of(me * rows_dev, rows_dev)
 
@@ -224,9 +230,18 @@
         cos_tab[r * draft : (r + 1) * draft, :] = jnp.cos(angle)
         sin_tab[r * draft : (r + 1) * draft, :] = jnp.sin(angle) * half_sign
     hops = []
+    tile = 512
+    loads[3].wait()
     if grid4:
         gathers[1].wait_send()
         gathers[2].start()
+
+    @pl.loop(0, width // tile)
+    def _(i):
+        c = pl.ds(pl.multiple_of(i * tile, tile), tile)
+        w_out_t[:, c] = w_out[c, :].T
+
+    if grid4:
         gathers[1].wait_recv()
         held = block(rows, dst_chip(first) * 2 + core)
         hops.append(
@@ -236,7 +251,7 @@
             )
         )
         hops[0].start()
-    for load in loads[:4]:
+    for load in loads[:3]:
         load.wait()
 
     scale = 1.0 / math.sqrt(head)
@@ -305,13 +320,11 @@
             attn.append((summed / total).astype(BF16))
         attn = jnp.concatenate(attn, axis=0)
 
-        tile = 512
-
         @pl.loop(0, width // tile)
         def _(i):
             c = pl.ds(pl.multiple_of(i * tile, tile), tile)
-            terms[span, c] = lax.dot_general(
-                attn, w_out[c, :], nt, preferred_element_type=F32
+            terms[span, c] = jnp.dot(
+                attn, w_out_t[:, c], preferred_element_type=F32
             ).astype(BF16)
 
         return (p, k, v, ancestry)
@@ -476,7 +489,7 @@
     lane = jnp.arange(head, dtype=jnp.int32) % (head // 2)
     freq = (rope_base ** (-(lane.astype(F32) * 2.0 / head)))[None, :]
     vmem = pl.BlockSpec(memory_space=pltpu.VMEM)
-    hbm = pl.BlockSpec(memory_space=pl.ANY)
+    hbm = pl.BlockSpec(memory_space=pltpu.HBM)
     dma = pltpu.SemaphoreType.DMA
     page = kv_pool.shape[1]
     return pl.pallas_call(
@@ -485,7 +498,7 @@
             jax.ShapeDtypeStruct((rows_dev, width), BF16),
             jax.ShapeDtypeStruct((slots, draft, 2 * head), BF16),
         ),
-        in_specs=[vmem] * 6 + [hbm] * 9,
+        in_specs=[vmem] * 4 + [hbm] * 2 + [pl.BlockSpec(memory_space=pl.ANY)] * 5 + [hbm] * 4,
         out_specs=(vmem, vmem),
         scratch_shapes=[
             pltpu.VMEM((count, width), BF16),
@@ -503,25 +516,28 @@
             pltpu.SMEM(migrate_to.shape, jnp.int32),
             pltpu.SMEM(leave_slot.shape, jnp.int32),
             pltpu.VMEM((slots // 2, 1, 2 * draft), jnp.int32),
+            pltpu.VMEM((rows_dev, width), BF16),
+            pltpu.VMEM(kv_pool.shape, BF16),
+            pltpu.VMEM((head, width), BF16),
             pltpu.VMEM((count, width), BF16),
             pltpu.VMEM((chips, rows_dev, width), BF16),
             pltpu.VMEM((chips, rows_dev, width), BF16),
             pltpu.VMEM((chips, rows_dev, width), BF16),
-            dma((10,)),
+            dma((12,)),
         ]
         + [dma((chips,))] * 6
         + [dma((chips + 2,))] * 2
         + [dma((reps,))] * 4,
         compiler_params=pltpu.CompilerParams(
-            collective_id=0, has_side_effects=True, vmem_limit_bytes=48 * 1024 * 1024
+            collective_id=0, has_side_effects=True, vmem_limit_bytes=60 * 1024 * 1024
         ),
     )(
-        hidden,
         norm_gain[None, :],
-        kv_pool,
         parents,
         depths,
         freq,
+        hidden,
+        kv_pool,
         page_table,
         cache_len,
         accept_node,

time: 62.4 us -> 59.3 us (0.950)
  local copies, waits for them, and re-layouts: 10 us -> 4.68 us
  Pallas kernels: 51.2 us -> 53.1 us
    unnamed x29 -> x7, local copies, waits for them, and re-layouts: 9.24 us -> 3.37 us
    pallas_call x1, Pallas kernels: 51.2 us -> 53.1 us  [local(): pl.pallas_call(functools.partial(kernel, n, reps), out_shape=(jax.ShapeDt...]
where the time goes in v3:
time: 59.3 us; the launch traced here: 59 us
  Pallas kernels  53.1 us (90%)
  local copies, waits for them, and re-layouts  4.68 us (8%)
  between operations  0.66 us (1%)
    pallas_call x1, Pallas kernels, local(): pl.pallas_call(functools.partial(kernel, n, reps), out_shape=(jax.ShapeDt...  53.1 us
    unnamed x7, local copies, waits for them, and re-layouts  3.37 us
    broadcast_in_dim x1, local copies, waits for them, and re-layouts, local(): norm_gain[None, :]  1.31 us

profile of v3, /device:TPU:0, one launch (start us, length us, event | category | flops | bytes accessed | tf_op | source)
XLA Modules:
  0.0 59.0 jit_solution(13213854028546547564)
XLA Ops:
  0.6 0.0 copy-start.1
  0.6 0.6 fusion.3.freq
  1.2 0.1 copy-done.1
  1.3 0.7 %copy.16.page_table_in = s32[8,2]{1,0:T(8,128)} copy(s32[8,2]{0,1:T(2,128)S(1)} %copy-done.1) | data formatting | bytes 128 | tf_op args[7]
  2.0 1.3 %broadcast_in_dim.4.gain = bf16[1,4096]{1,0:T(2,128)(2,1)} reshape(bf16[4096]{0:T(1024)(128)(2,1)} %param.15) | data formatting | bytes 16384 | tf_op jit(solution)/shard_map/broadcast_in_dim | solution.py:535
  3.3 53.1 %shard_map.149 = (bf16[64,4096]{1,0:T(8,128)(2,1)}, bf16[8,64,256]{2,1,0:T(8,128)(2,1)}) custom-call(bf16[1,4096]{1,0:T(2,128)(2,1)} %broadcast_in_dim.4.gain, s32[8,64]{1,0:T(8,128)} %parents.1, s32[8,64]{1,0:T(8,128)} %depths.1, f32[1,128]{1,0:T(1,128)} %fusion.3.freq, bf16[64,4096]{1,0:T(8,128)(2,1)} %hidden_in.1, bf16[16,64,256]{2,1,0:T(8,128)(2,1)} %pool_in.1, ...), custom_call_target="tpu_custom_call" | custom-call | tf_op jit(solution)/shard_map/pallas_call | solution.py:495
  56.4 0.0 copy-start
  56.4 1.9 %copy.19 = bf16[64,4096]{1,0:T(8,128)(2,1)} copy(bf16[64,4096]{1,0:T(8,128)(2,1)} %get-tuple-element.4) | data formatting | bytes 1048576
  58.3 0.0 copy-done
  58.3 0.7 %copy.20 = bf16[8,64,256]{2,1,0:T(8,128)(2,1)} copy(bf16[8,64,256]{2,1,0:T(8,128)(2,1)S(1)} %copy-done) | data formatting | bytes 524288
Async XLA Ops:
  0.6 0.7 %copy-start.1 = (s32[8,2]{0,1:T(2,128)S(1)}, s32[8,2]{0,1:T(2,128)}, u32[]{:S(2)}) copy-start(s32[8,2]{0,1:T(2,128)} %param.21) | copy-start | bytes 196
  56.4 1.9 %copy-start = (bf16[8,64,256]{2,1,0:T(8,128)(2,1)S(1)}, bf16[8,64,256]{2,1,0:T(8,128)(2,1)}, u32[]{:S(2)}) copy-start(bf16[8,64,256]{2,1,0:T(8,128)(2,1)} %get-tuple-element.5) | copy-start | bytes 786436

commit v4 on v3

--- a/solution.py
+++ b/solution.py
@@ -21,7 +21,6 @@
     gain,
     parents,
     depths,
-    freq,
     hidden_in,
     pool_in,
     page_table_in,
@@ -137,13 +136,14 @@
         load.start()
     load_hidden.wait()
 
+    gain_row = gain[...].astype(F32).reshape(1, width)
     own = pl.multiple_of(me * rows_dev, rows_dev)
 
     @pl.loop(0, rows_dev // 16)
     def _(i):
         x = hidden[pl.ds(pl.multiple_of(i * 16, 16), 16), :].astype(F32)
         mean = jnp.mean(x * x, axis=-1, keepdims=True)
-        y = x * lax.rsqrt(mean + eps) * gain[...].astype(F32)
+        y = x * lax.rsqrt(mean + eps) * gain_row
         rows[pl.ds(pl.multiple_of(own + i * 16, 16), 16), :] = y.astype(BF16)
 
     for load in small:
@@ -216,6 +216,8 @@
     source = jnp.int32(0)
     for g in range(reps):
         source = jnp.where(migrate_to[g] == rep, g, source)
+    lane = lax.broadcasted_iota(jnp.int32, (1, head), 1) % (head // 2)
+    freq = jnp.exp(lane.astype(F32) * (-2.0 / head * math.log(rope_base)))
     came = moved_len[source][0:1, :]
     half_sign = jnp.where(
         lax.broadcasted_iota(jnp.int32, (1, head), 1) < head // 2, -1.0, 1.0
@@ -226,7 +228,7 @@
         new_len[r] = length
         at = slice(r % 2 * draft, (r % 2 + 1) * draft)
         place = length.astype(F32) + place_col[r // 2][at]
-        angle = place * freq[...]
+        angle = place * freq
         cos_tab[r * draft : (r + 1) * draft, :] = jnp.cos(angle)
         sin_tab[r * draft : (r + 1) * draft, :] = jnp.sin(angle) * half_sign
     hops = []
@@ -486,8 +488,6 @@
     head = w_query.shape[1]
     count = slots * draft
     chips = n // 2
-    lane = jnp.arange(head, dtype=jnp.int32) % (head // 2)
-    freq = (rope_base ** (-(lane.astype(F32) * 2.0 / head)))[None, :]
     vmem = pl.BlockSpec(memory_space=pltpu.VMEM)
     hbm = pl.BlockSpec(memory_space=pltpu.HBM)
     dma = pltpu.SemaphoreType.DMA
@@ -498,7 +498,7 @@
             jax.ShapeDtypeStruct((rows_dev, width), BF16),
             jax.ShapeDtypeStruct((slots, draft, 2 * head), BF16),
         ),
-        in_specs=[vmem] * 4 + [hbm] * 2 + [pl.BlockSpec(memory_space=pl.ANY)] * 5 + [hbm] * 4,
+        in_specs=[vmem] * 3 + [hbm] * 2 + [pl.BlockSpec(memory_space=pl.ANY)] * 5 + [hbm] * 4,
         out_specs=(vmem, vmem),
         scratch_shapes=[
             pltpu.VMEM((count, width), BF16),
@@ -532,10 +532,9 @@
             collective_id=0, has_side_effects=True, vmem_limit_bytes=60 * 1024 * 1024
         ),
     )(
-        norm_gain[None, :],
+        norm_gain,
         parents,
         depths,
-        freq,
         hidden,
         kv_pool,
         page_table,

time: 59.3 us -> 57.9 us (0.976)
  local copies, waits for them, and re-layouts: 4.68 us -> 3.96 us
    broadcast_in_dim x1 -> x0, local copies, waits for them, and re-layouts: 1.31 us -> none  [local(): norm_gain[None, :]]
    unnamed x7 -> x5, local copies, waits for them, and re-layouts: 3.37 us -> 3.96 us
where the time goes in v4:
time: 57.9 us; the launch traced here: 57.7 us
  Pallas kernels  53 us (92%)
  local copies, waits for them, and re-layouts  3.96 us (7%)
  between operations  0.65 us (1%)
    pallas_call x1, Pallas kernels, local(): pl.pallas_call(functools.partial(kernel, n, reps), out_shape=(jax.ShapeDt...  53 us
    unnamed x5, local copies, waits for them, and re-layouts  3.96 us

profile of v4, /device:TPU:0, one launch (start us, length us, event | category | flops | bytes accessed | tf_op | source)
XLA Modules:
  0.0 57.7 jit_solution(4656311451163198252)
XLA Ops:
  0.6 1.3 %copy.16.page_table_in = s32[8,2]{1,0:T(8,128)} copy(s32[8,2]{0,1:T(2,128)} %param.21) | data formatting | bytes 128 | tf_op args[7]
  2.0 53.0 %shard_map.149 = (bf16[64,4096]{1,0:T(8,128)(2,1)}, bf16[8,64,256]{2,1,0:T(8,128)(2,1)}) custom-call(bf16[4096]{0:T(1024)(128)(2,1)} %gain.1, s32[8,64]{1,0:T(8,128)} %parents.1, s32[8,64]{1,0:T(8,128)} %depths.1, bf16[64,4096]{1,0:T(8,128)(2,1)} %hidden_in.1, bf16[16,64,256]{2,1,0:T(8,128)(2,1)} %pool_in.1, s32[8,2]{1,0:T(8,128)} %copy.16.page_table_in, ...), custom_call_target="tpu_custom_call" | custom-call | tf_op jit(solution)/shard_map/pallas_call | solution.py:495
  55.0 0.0 copy-start
  55.0 1.9 %copy.19 = bf16[64,4096]{1,0:T(8,128)(2,1)} copy(bf16[64,4096]{1,0:T(8,128)(2,1)} %get-tuple-element.4) | data formatting | bytes 1048576
  56.9 0.0 copy-done
  56.9 0.7 %copy.20 = bf16[8,64,256]{2,1,0:T(8,128)(2,1)} copy(bf16[8,64,256]{2,1,0:T(8,128)(2,1)S(1)} %copy-done) | data formatting | bytes 524288
Async XLA Ops:
  55.0 1.9 %copy-start = (bf16[8,64,256]{2,1,0:T(8,128)(2,1)S(1)}, bf16[8,64,256]{2,1,0:T(8,128)(2,1)}, u32[]{:S(2)}) copy-start(bf16[8,64,256]{2,1,0:T(8,128)(2,1)} %get-tuple-element.5) | copy-start | bytes 786436
